TPU v7x, 128 devices: a whole 4x4x4 slice. The times are simulated.
128 devices in a mesh: seq: 128 (over y, x, z, core).
Axes of the slice: x: 4, y: 4, z: 4, core: 2. Of those that a mesh axis runs over, the one named last changes fastest.
Arguments:
- queries: bfloat16 [524288, 768], P('seq'), may hold values from -8 to 8
- key_rows: bfloat16 [524288, 768], P('seq'), may hold values from -8 to 8
- value_rows: bfloat16 [524288, 768], P('seq'), may hold values from -6 to 6
Outputs:
- mixed: bfloat16 [524288, 768], P('seq')
All inputs are finite; a program needn't handle non-finite values.
Results may differ from a plain program's by a relative error of at most 0.0037.
Values may be sent and summed in bfloat16 or wider, within the bound.
No kernel may reach another device: no remote copies, remote signals or barrier semaphores. Data moves between devices by JAX's collectives and lax.ppermute only.
A program may use at most 128 MiB of HBM per device.

v0:
```python
import jax
import jax.numpy as jnp
from jax import lax
from jax.experimental import pallas as pl
from jax.experimental.pallas import tpu as pltpu
from jax.sharding import PartitionSpec as P

HEADS = 12
HEAD = 64
PAIR = 2 * HEAD
BLOCK = 512
TILE = 128
TILES = BLOCK // TILE
PAIRS = HEADS // 2
WIDTH = HEADS * HEAD
ROWS = 16
STRIDE = 256
UNIT = 2 * ROWS
VMEM = 52 << 20
LOCAL_VMEM = 52 << 20
MERGE_VMEM = 20 << 20

MASKED = -1e30
BF16 = jnp.bfloat16
F32 = jnp.float32
TRANSPOSED = (((1,), (1,)), ((), ()))

CHUNKS = (2, 5, 1)


def owner_mask(rows, row_size, columns):
    row = lax.broadcasted_iota(jnp.int32, (rows, columns), 0) // row_size
    head = lax.broadcasted_iota(jnp.int32, (rows, columns), 1) // HEAD
    return row == head


def pick_kernel(q_ref, k_ref, v_ref, q_out, own_out, second_out, fourth_out):
    owned = owner_mask(ROWS, 1, WIDTH)

    def diagonal(ref):
        return [
            jnp.sum(jnp.where(owned, ref[i].astype(F32), 0.0), axis=0, keepdims=True)
            for i in range(ROWS)
        ]

    def pack(rows):
        return jnp.concatenate(rows, 0).astype(BF16)

    q_out[...] = pack(diagonal(q_ref))
    for ref, columns in ((k_ref, slice(0, WIDTH)), (v_ref, slice(WIDTH, 2 * WIDTH))):
        rows = diagonal(ref)
        none = [jnp.zeros_like(rows[0])] * (ROWS // 4)
        own_out[:, columns] = pack(rows)
        second_out[:, columns] = pack(rows[2::4] + rows[::4])
        fourth_out[:, columns] = pack(rows[::4] + none)


def pick(queries, key_rows, value_rows):
    spec = pl.BlockSpec((ROWS, ROWS, WIDTH), lambda i: (0, 0, 0))
    shape = (ROWS, STRIDE, WIDTH)
    outs = [
        jax.ShapeDtypeStruct(size, BF16)
        for size in ((ROWS, WIDTH), (ROWS, 2 * WIDTH)) + ((ROWS // 2, 2 * WIDTH),) * 2
    ]
    return pl.pallas_call(
        pick_kernel,
        grid=(1,),
        in_specs=[spec] * 3,
        out_specs=[pl.BlockSpec(out.shape, lambda i: (0, 0)) for out in outs],
        out_shape=outs,
        compiler_params=pltpu.CompilerParams(vmem_limit_bytes=VMEM),
        name="pick",
    )(queries.reshape(shape), key_rows.reshape(shape), value_rows.reshape(shape))


def local_kernel(q_ref, k_ref, v_ref, *refs):
    out_ref, kept_ref = refs[-2:]
    low = lax.broadcasted_iota(jnp.int32, (1, PAIR), 1) < HEAD
    keep = lax.broadcasted_iota(
        jnp.int32, (TILE, 2 * TILE), 1
    ) % TILE <= lax.broadcasted_iota(jnp.int32, (TILE, 2 * TILE), 0)
    zero = jnp.zeros((TILE, PAIR), BF16)
    one = jnp.ones((TILE, PAIR), BF16)
    counters = jnp.where(low, one, zero), jnp.where(low, zero, one)

    def columns(pair):
        return slice(pair * PAIR, (pair + 1) * PAIR)

    def score(pair, j):
        query = q_ref[j * TILE :, columns(pair)] * jnp.asarray(HEAD**-0.5, BF16)
        key = k_ref[j * TILE : (j + 1) * TILE, columns(pair)]
        both = jnp.concatenate([jnp.where(low, key, zero), jnp.where(low, zero, key)], 0)
        return lax.dot_general(query, both, TRANSPOSED, preferred_element_type=F32)

    def soften(scores, t):
        parts = [scores[j][(t - j) * TILE : (t - j + 1) * TILE] for j in range(t + 1)]
        parts[t] = jnp.where(keep, parts[t], MASKED)
        most = parts[0]
        for part in parts[1:]:
            most = jnp.maximum(most, part)
        tops = [
            jnp.broadcast_to(
                jnp.max(most[:, start : start + TILE], axis=1, keepdims=True), (TILE, TILE)
            )
            for start in (0, TILE)
        ]
        top = jnp.concatenate(tops, 1)
        return jnp.concatenate([jnp.exp(part - top).astype(BF16) for part in parts], 1), tops

    def finish(pair, t, probs, tops):
        weights = []
        for j in range(t + 1):
            value = v_ref[j * TILE : (j + 1) * TILE, columns(pair)]
            weights.append(jnp.concatenate([jnp.where(low, value, zero), counters[0]], 1))
            weights.append(jnp.concatenate([jnp.where(low, zero, value), counters[1]], 1))
        both = jnp.dot(probs, jnp.concatenate(weights, 0), preferred_element_type=F32)
        upper, lower = both[:, :PAIR], both[:, PAIR:]
        out_ref[t * TILE : (t + 1) * TILE, columns(pair)] = (upper / lower).astype(BF16)
        if t * TILE % STRIDE == 0:
            a, b = 2 * pair, 2 * pair + 1
            for start, (x, y) in ((0, (upper, upper)), (2, (lower, lower)), (4, tops)):
                row = start + t * TILE // STRIDE
                kept_ref[row : row + 1, columns(pair)] = jnp.where(
                    low, x[a : a + 1], y[b : b + 1]
                )

    ready = [score(0, j) for j in range(TILES)]
    waiting = []
    for pair in range(PAIRS):
        later = []
        for t in range(TILES):
            if pair + 1 < PAIRS:
                later.append(score(pair + 1, t))
            waiting.append((pair, t, *soften(ready, t)))
            if len(waiting) > 1:
                finish(*waiting.pop(0))
        ready = later
    finish(*waiting.pop(0))


def local_level(first, count, arrays, complete):
    spec = pl.BlockSpec((BLOCK, WIDTH), lambda i: (first + i, 0))
    operands = list(arrays)
    in_specs = [spec] * 3
    aliases = {}
    if complete is not None:
        operands.append(complete)
        in_specs.append(pl.BlockSpec(memory_space=pl.ANY))
        aliases = {3: 0}
    return pl.pallas_call(
        local_kernel,
        grid=(count,),
        in_specs=in_specs,
        out_specs=[spec, pl.BlockSpec((8, WIDTH), lambda i: (i, 0))],
        out_shape=[
            jax.ShapeDtypeStruct(arrays[0].shape, BF16),
            jax.ShapeDtypeStruct((8 * count, WIDTH), F32),
        ],
        input_output_aliases=aliases,
        compiler_params=pltpu.CompilerParams(vmem_limit_bytes=LOCAL_VMEM),
        cost_estimate=pl.CostEstimate(
            flops=count * HEADS * 4 * BLOCK * BLOCK * HEAD * 4,
            bytes_accessed=count * 8 * BLOCK * WIDTH,
            transcendentals=count * HEADS * BLOCK * BLOCK,
        ),
        name="local",
    )(*operands)


def merge_kernel(spot_ref, q_ref, own_ref, other_ref, *refs):
    kept_refs, old_ref, out_ref, corner, sems = refs[:-5], refs[-5], refs[-4], refs[-3], refs[-2:]
    old = pltpu.make_async_copy(old_ref.at[:, pl.ds(0, ROWS), :], corner, sems[0])
    old.start()
    lanes = HEADS * ROWS
    owned = owner_mask(lanes, ROWS, WIDTH)
    query = q_ref[...] * jnp.asarray(HEAD**-0.5, BF16)
    spread = jnp.where(owned, jnp.concatenate([query] * HEADS, 0), jnp.zeros((), BF16))
    score = jnp.concatenate(
        [
            lax.dot_general(spread, ref[:, :WIDTH], TRANSPOSED, preferred_element_type=F32)
            for ref in (own_ref, other_ref)
        ],
        1,
    )
    keys = score.shape[1]
    device = spot_ref[0]
    column = lax.broadcasted_iota(jnp.int32, (1, keys), 1)
    core, x, z = column // (keys // 2), column // (4 * UNIT) % 4, column // UNIT % 4
    inner = column % UNIT
    quarter = jnp.where(inner < 16, 0, jnp.where(inner < 24, 1, jnp.where(inner < 28, 3, 2)))
    index = jnp.where(
        inner < 16, inner, 4 * (inner % 4) + jnp.where((inner >= 16) & (inner < 20), 2, 0)
    )
    source = jnp.bitwise_xor(device, quarter * 32 + x * 8 + z * 2 + core)
    key_place = source * ROWS + index
    row = lax.broadcasted_iota(jnp.int32, (lanes, 1), 0) % ROWS
    query_place = device * ROWS + row
    in_one = (quarter == 0).astype(F32)
    in_two = jnp.where((quarter <= 1) & (index % 2 == 0), 1.0, 0.0)
    in_three = jnp.where(index % 4 == 0, 1.0, 0.0)
    has_two = jnp.where(row % 2 == 0, 1.0, 0.0)
    has_three = jnp.where(row % 4 == 0, 1.0, 0.0)
    count = in_one + has_two * in_two + has_three * in_three
    count = jnp.where(key_place <= query_place, count, 0.0)
    score = jnp.where(count > 0.0, score, MASKED)
    top = jnp.max(score, axis=1, keepdims=True)
    probs = jnp.exp(score - top) * count
    total = jnp.sum(probs, axis=1, keepdims=True)
    probs = probs.astype(BF16)
    result = jnp.dot(probs[:, : keys // 2], own_ref[:, WIDTH:], preferred_element_type=F32)
    result = result + jnp.dot(
        probs[:, keys // 2 :], other_ref[:, WIDTH:], preferred_element_type=F32
    )

    def gather_heads(array):
        kept = jnp.where(owned, array, 0.0)
        return jnp.sum(kept.reshape(HEADS, ROWS, WIDTH), axis=0)

    top, total, result = gather_heads(top), gather_heads(total), gather_heads(result)
    blocks = [ref[8 * i : 8 * i + 8] for ref in kept_refs for i in range(ref.shape[0] // 8)]
    result_zero, total_zero, top_zero = (
        jnp.concatenate([block[start : start + 2] for block in blocks], 0) for start in (0, 2, 4)
    )
    best = jnp.maximum(top, top_zero)
    weight, weight_zero = jnp.exp(top - best), jnp.exp(top_zero - best)
    mixed = (weight * result + weight_zero * result_zero) / (
        weight * total + weight_zero * total_zero
    )
    owned = owner_mask(ROWS, 1, WIDTH)
    old.wait()
    for i in range(ROWS):
        corner[i] = jnp.where(owned, mixed[i : i + 1], corner[i].astype(F32)).astype(BF16)
    new = pltpu.make_async_copy(corner, out_ref.at[:, pl.ds(0, ROWS), :], sems[1])
    new.start()
    new.wait()


def merge(spot, query, own, other, kept, complete):
    shape = (ROWS, STRIDE, WIDTH)
    held = pl.BlockSpec(memory_space=pltpu.VMEM)
    anywhere = pl.BlockSpec(memory_space=pl.ANY)
    merged = pl.pallas_call(
        merge_kernel,
        in_specs=[pl.BlockSpec(memory_space=pltpu.SMEM)] + [held] * (3 + len(kept)) + [anywhere],
        out_specs=anywhere,
        out_shape=jax.ShapeDtypeStruct(shape, BF16),
        input_output_aliases={4 + len(kept): 0},
        scratch_shapes=[
            pltpu.VMEM((ROWS, ROWS, WIDTH), BF16),
            pltpu.SemaphoreType.DMA,
            pltpu.SemaphoreType.DMA,
        ],
        compiler_params=pltpu.CompilerParams(vmem_limit_bytes=MERGE_VMEM),
        name="merge",
    )(spot, query, own, other, *kept, complete.reshape(shape))
    return merged.reshape(complete.shape)


def local(queries, key_rows, value_rows):
    devices = lax.axis_size("seq")
    arrays = (queries, key_rows, value_rows)

    def exchange(array, distance):
        return lax.ppermute(array, "seq", [(i, i ^ distance) for i in range(devices)])

    query, rows, second, fourth = pick(*arrays)
    near = exchange(second, 32)
    own = lax.broadcasted_iota(jnp.int32, second.shape, 0) < ROWS // 4
    far = exchange(jnp.where(own, fourth, near), 96)
    rows = jnp.concatenate([rows, near, far], 0)
    complete, kept, first = None, [], 0
    for stage, (distances, count) in enumerate(zip(((2, 4, 6), (8, 16, 24), (1,)), CHUNKS)):
        rows, complete, arrays = lax.optimization_barrier((rows, complete, arrays))
        received = [exchange(rows, distance) for distance in distances]
        complete, some = local_level(first, count, arrays, complete)
        first += count
        kept.append(some)
        received, rows, complete = lax.optimization_barrier((received, rows, complete))
        if stage < 2:
            rows = jnp.concatenate([rows, *received], 0)
    spot = lax.axis_index("seq").astype(jnp.int32).reshape(1)
    return merge(spot, query, rows, received[0], kept, complete)


def solution(mesh):
    in_specs = (P("seq", None), P("seq", None), P("seq", None))
    out_specs = P("seq", None)
    return jax.shard_map(local, mesh=mesh, in_specs=in_specs, out_specs=out_specs, check_vma=False)
```

profile of v0, /device:TPU:1, one launch (start us, length us, event | category | flops | bytes accessed | tf_op | source)
XLA Modules:
  0.0 54.2 jit_solution(8213406957059528810)
XLA Ops:
  0.0 1.6 %pick.1 = (bf16[16,768]{1,0:T(8,128)(2,1)S(1)}, bf16[16,1536]{1,0:T(8,128)(2,1)S(1)}, bf16[8,1536]{1,0:T(8,128)(2,1)S(1)}, bf16[8,1536]{1,0:T(8,128)(2,1)S(1)}) custom-call(bf16[16,256,768]{2,1,0:T(8,128)(2,1)} %bitcast.7, bf16[16,256,768]{2,1,0:T(8,128)(2,1)} %bitcast.8, bf16[16,256,768]{2,1,0:T(8,128)(2,1)} %bitcast.9), custom_call_target="tpu_custom_call" | custom-call | tf_op jit(solution)/shard_map/pick/pallas_call | solution.py:65
  1.6 2.2 %collective-permute-start = (bf16[8,1536]{1,0:T(8,128)(2,1)S(1)}, bf16[8,1536]{1,0:T(8,128)(2,1)S(1)}, u32[]{:S(2)}, u32[]{:S(2)}) collective-permute-start(bf16[8,1536]{1,0:T(8,128)(2,1)S(1)} %get-tuple-element.44), channel_id=1, source_target_pairs={{0,32},{1,33},{2,34},{3,35},{4,36},{5,37},{6,38},{7,39},{8,40},{9,... | collective-permute-start | bytes 73736 | tf_op jit(solution)/shard_map/ppermute | solution.py:264
  3.8 1.2 %collective-permute-done = bf16[8,1536]{1,0:T(8,128)(2,1)S(1)} collective-permute-done((bf16[8,1536]{1,0:T(8,128)(2,1)S(1)}, bf16[8,1536]{1,0:T(8,128)(2,1)S(1)}, u32[]{:S(2)}, u32[]{:S(2)}) %collective-permute-start) | collective-permute-done | bytes 24608 | tf_op jit(solution)/shard_map/ppermute | solution.py:264
  5.1 0.1 broadcast_select_fusion
  5.1 2.9 %collective-permute-start.1 = (bf16[8,1536]{1,0:T(8,128)(2,1)S(1)}, bf16[8,1536]{1,0:T(8,128)(2,1)S(1)}, u32[]{:S(2)}, u32[]{:S(2)}) collective-permute-start(bf16[8,1536]{1,0:T(8,128)(2,1)S(1)} %broadcast_select_fusion), channel_id=1, source_target_pairs={{0,96},{1,97},{2,98},{3,99},{4,100},{5,101},{6,102},{7,103},{8,104... | collective-permute-start | bytes 73736 | tf_op jit(solution)/shard_map/ppermute | solution.py:264
  8.0 1.2 %collective-permute-done.1 = bf16[8,1536]{1,0:T(8,128)(2,1)S(1)} collective-permute-done((bf16[8,1536]{1,0:T(8,128)(2,1)S(1)}, bf16[8,1536]{1,0:T(8,128)(2,1)S(1)}, u32[]{:S(2)}, u32[]{:S(2)}) %collective-permute-start.1) | collective-permute-done | bytes 24608 | tf_op jit(solution)/shard_map/ppermute | solution.py:264
  9.3 3.8 %collective-permute-start.4 = (bf16[32,1536]{1,0:T(8,128)(2,1)S(1)}, bf16[32,1536]{1,0:T(8,128)(2,1)S(1)}, u32[]{:S(2)}, u32[]{:S(2)}) collective-permute-start(bf16[32,1536]{1,0:T(8,128)(2,1)S(1)} %pad_maximum_fusion.2), channel_id=1, source_target_pairs={{0,6},{1,7},{2,4},{3,5},{4,2},{5,3},{6,0},{7,1},{8,14},{9,15},{10,... | collective-permute-start | bytes 294920 | tf_op jit(solution)/shard_map/ppermute | solution.py:264
  13.1 0.0 collective-permute-start.3
  13.1 0.7 %collective-permute-start.2 = (bf16[32,1536]{1,0:T(8,128)(2,1)S(1)}, bf16[32,1536]{1,0:T(8,128)(2,1)S(1)}, u32[]{:S(2)}, u32[]{:S(2)}) collective-permute-start(bf16[32,1536]{1,0:T(8,128)(2,1)S(1)} %pad_maximum_fusion.2), channel_id=1, source_target_pairs={{0,2},{1,3},{2,0},{3,1},{4,6},{5,7},{6,4},{7,5},{8,10},{9,11},{10,... | collective-permute-start | bytes 294920 | tf_op jit(solution)/shard_map/ppermute | solution.py:264
  13.8 8.1 %local.3 = (bf16[4096,768]{1,0:T(8,128)(2,1)}, f32[16,768]{1,0:T(8,128)S(1)}) custom-call(bf16[4096,768]{1,0:T(8,128)(2,1)} %q_ref.2, bf16[4096,768]{1,0:T(8,128)(2,1)} %k_ref.2, bf16[4096,768]{1,0:T(8,128)(2,1)} %v_ref.2), custom_call_target="tpu_custom_call" | custom-call | flops 6442450944 | bytes 6291456 | tf_op jit(solution)/shard_map/local/pallas_call | solution.py:150
  21.9 0.0 collective-permute-done.4
  21.9 0.0 collective-permute-done.3
  21.9 0.0 collective-permute-done.2
  21.9 2.6 %collective-permute-start.7 = (bf16[128,1536]{1,0:T(8,128)(2,1)S(1)}, bf16[128,1536]{1,0:T(8,128)(2,1)S(1)}, u32[]{:S(2)}, u32[]{:S(2)}) collective-permute-start(bf16[128,1536]{1,0:T(8,128)(2,1)S(1)} %pad_maximum_fusion.1), channel_id=1, source_target_pairs={{0,24},{1,25},{2,26},{3,27},{4,28},{5,29},{6,30},{7,31},{8,16},{9,... | collective-permute-start | bytes 1179656 | tf_op jit(solution)/shard_map/ppermute | solution.py:264
  24.5 0.5 collective-permute-start.6
  25.0 0.3 collective-permute-start.5
  25.3 16.5 %local.4 = (bf16[4096,768]{1,0:T(8,128)(2,1)}, f32[40,768]{1,0:T(8,128)S(1)}) custom-call(bf16[4096,768]{1,0:T(8,128)(2,1)} %q_ref.2, bf16[4096,768]{1,0:T(8,128)(2,1)} %k_ref.2, bf16[4096,768]{1,0:T(8,128)(2,1)} %v_ref.2, bf16[4096,768]{1,0:T(8,128)(2,1)} %get-tuple-element.60.refs_0_), custom_call_target="tpu_custom_call", output_to_operand_aliasing={{0}: (3, {})} | custom-call | flops 16106127360 | bytes 15728640 | tf_op jit(solution)/shard_map/local/pallas_call | solution.py:150
  41.8 0.0 collective-permute-done.7
  41.8 0.0 collective-permute-done.5
  41.8 0.1 pad_maximum_fusion.own_ref
  41.9 4.6 %collective-permute-start.8 = (bf16[512,1536]{1,0:T(8,128)(2,1)S(1)}, bf16[512,1536]{1,0:T(8,128)(2,1)S(1)}, u32[]{:S(2)}, u32[]{:S(2)}) collective-permute-start(bf16[512,1536]{1,0:T(8,128)(2,1)S(1)} %pad_maximum_fusion.own_ref), channel_id=1, source_target_pairs={{0,1},{1,0},{2,3},{3,2},{4,5},{5,4},{6,7},{7,6},{8,9},{9,8},{10,11... | collective-permute-start | bytes 4718600 | tf_op jit(solution)/shard_map/ppermute | solution.py:264
  46.5 5.3 %local.5 = (bf16[4096,768]{1,0:T(8,128)(2,1)}, f32[8,768]{1,0:T(8,128)S(1)}) custom-call(bf16[4096,768]{1,0:T(8,128)(2,1)} %q_ref.2, bf16[4096,768]{1,0:T(8,128)(2,1)} %k_ref.2, bf16[4096,768]{1,0:T(8,128)(2,1)} %v_ref.2, bf16[4096,768]{1,0:T(8,128)(2,1)} %get-tuple-element.71.refs_0_), custom_call_target="tpu_custom_call", output_to_operand_aliasing={{0}: (3, {})} | custom-call | flops 3221225472 | bytes 3145728 | tf_op jit(solution)/shard_map/local/pallas_call | solution.py:150
  51.7 0.0 collective-permute-done.8.other_ref
  51.8 2.3 %merge.1 = bf16[16,256,768]{2,1,0:T(8,128)(2,1)} custom-call(s32[1]{0:T(128)} %bitcast.spot_ref, bf16[16,768]{1,0:T(8,128)(2,1)S(1)} %get-tuple-element.42.q_ref, bf16[512,1536]{1,0:T(8,128)(2,1)S(1)} %pad_maximum_fusion.own_ref, bf16[512,1536]{1,0:T(8,128)(2,1)S(1)} %collective-permute-done.8.other_ref, ...), custom_call_target="tpu_custom_call", output_to_operand_aliasing={{}: (7, {})} | custom-call | tf_op jit(solution)/shard_map/merge/pallas_call | solution.py:242
  (4 shorter events, 0.0 us)
Async XLA Ops:
  1.6 3.4 %collective-permute-start = (bf16[8,1536]{1,0:T(8,128)(2,1)S(1)}, bf16[8,1536]{1,0:T(8,128)(2,1)S(1)}, u32[]{:S(2)}, u32[]{:S(2)}) collective-permute-start(bf16[8,1536]{1,0:T(8,128)(2,1)S(1)} %get-tuple-element.44), channel_id=1, source_target_pairs={{0,32},{1,33},{2,34},{3,35},{4,36},{5,37},{6,38},{7,39},{8,40},{9,... | collective-permute-start | bytes 73736 | tf_op jit(solution)/shard_map/ppermute | solution.py:264
  5.1 4.1 %collective-permute-start.1 = (bf16[8,1536]{1,0:T(8,128)(2,1)S(1)}, bf16[8,1536]{1,0:T(8,128)(2,1)S(1)}, u32[]{:S(2)}, u32[]{:S(2)}) collective-permute-start(bf16[8,1536]{1,0:T(8,128)(2,1)S(1)} %broadcast_select_fusion), channel_id=1, source_target_pairs={{0,96},{1,97},{2,98},{3,99},{4,100},{5,101},{6,102},{7,103},{8,104... | collective-permute-start | bytes 73736 | tf_op jit(solution)/shard_map/ppermute | solution.py:264
  9.3 12.6 %collective-permute-start.4 = (bf16[32,1536]{1,0:T(8,128)(2,1)S(1)}, bf16[32,1536]{1,0:T(8,128)(2,1)S(1)}, u32[]{:S(2)}, u32[]{:S(2)}) collective-permute-start(bf16[32,1536]{1,0:T(8,128)(2,1)S(1)} %pad_maximum_fusion.2), channel_id=1, source_target_pairs={{0,6},{1,7},{2,4},{3,5},{4,2},{5,3},{6,0},{7,1},{8,14},{9,15},{10,... | collective-permute-start | bytes 294920 | tf_op jit(solution)/shard_map/ppermute | solution.py:264
  13.1 8.8 %collective-permute-start.3 = (bf16[32,1536]{1,0:T(8,128)(2,1)S(1)}, bf16[32,1536]{1,0:T(8,128)(2,1)S(1)}, u32[]{:S(2)}, u32[]{:S(2)}) collective-permute-start(bf16[32,1536]{1,0:T(8,128)(2,1)S(1)} %pad_maximum_fusion.2), channel_id=1, source_target_pairs={{0,4},{1,5},{2,6},{3,7},{4,0},{5,1},{6,2},{7,3},{8,12},{9,13},{10,... | collective-permute-start | bytes 294920 | tf_op jit(solution)/shard_map/ppermute | solution.py:264
  13.1 8.8 %collective-permute-start.2 = (bf16[32,1536]{1,0:T(8,128)(2,1)S(1)}, bf16[32,1536]{1,0:T(8,128)(2,1)S(1)}, u32[]{:S(2)}, u32[]{:S(2)}) collective-permute-start(bf16[32,1536]{1,0:T(8,128)(2,1)S(1)} %pad_maximum_fusion.2), channel_id=1, source_target_pairs={{0,2},{1,3},{2,0},{3,1},{4,6},{5,7},{6,4},{7,5},{8,10},{9,11},{10,... | collective-permute-start | bytes 294920 | tf_op jit(solution)/shard_map/ppermute | solution.py:264
  21.9 19.9 %collective-permute-start.7 = (bf16[128,1536]{1,0:T(8,128)(2,1)S(1)}, bf16[128,1536]{1,0:T(8,128)(2,1)S(1)}, u32[]{:S(2)}, u32[]{:S(2)}) collective-permute-start(bf16[128,1536]{1,0:T(8,128)(2,1)S(1)} %pad_maximum_fusion.1), channel_id=1, source_target_pairs={{0,24},{1,25},{2,26},{3,27},{4,28},{5,29},{6,30},{7,31},{8,16},{9,... | collective-permute-start | bytes 1179656 | tf_op jit(solution)/shard_map/ppermute | solution.py:264
  24.5 17.3 %collective-permute-start.6 = (bf16[128,1536]{1,0:T(8,128)(2,1)S(1)}, bf16[128,1536]{1,0:T(8,128)(2,1)S(1)}, u32[]{:S(2)}, u32[]{:S(2)}) collective-permute-start(bf16[128,1536]{1,0:T(8,128)(2,1)S(1)} %pad_maximum_fusion.1), channel_id=1, source_target_pairs={{0,16},{1,17},{2,18},{3,19},{4,20},{5,21},{6,22},{7,23},{8,24},{9,... | collective-permute-start | bytes 1179656 | tf_op jit(solution)/shard_map/ppermute | solution.py:264
  25.0 16.8 %collective-permute-start.5 = (bf16[128,1536]{1,0:T(8,128)(2,1)S(1)}, bf16[128,1536]{1,0:T(8,128)(2,1)S(1)}, u32[]{:S(2)}, u32[]{:S(2)}) collective-permute-start(bf16[128,1536]{1,0:T(8,128)(2,1)S(1)} %pad_maximum_fusion.1), channel_id=1, source_target_pairs={{0,8},{1,9},{2,10},{3,11},{4,12},{5,13},{6,14},{7,15},{8,0},{9,1},... | collective-permute-start | bytes 1179656 | tf_op jit(solution)/shard_map/ppermute | solution.py:264
  41.9 9.8 %collective-permute-start.8 = (bf16[512,1536]{1,0:T(8,128)(2,1)S(1)}, bf16[512,1536]{1,0:T(8,128)(2,1)S(1)}, u32[]{:S(2)}, u32[]{:S(2)}) collective-permute-start(bf16[512,1536]{1,0:T(8,128)(2,1)S(1)} %pad_maximum_fusion.own_ref), channel_id=1, source_target_pairs={{0,1},{1,0},{2,3},{3,2},{4,5},{5,4},{6,7},{7,6},{8,9},{9,8},{10,11... | collective-permute-start | bytes 4718600 | tf_op jit(solution)/shard_map/ppermute | solution.py:264
where the time goes:
time: 54.4 us; the launch traced here: 54.2 us
  Pallas kernels  33.8 us (62%)
  starting transfers between devices  17.5 us (32%)
  waiting for transfers between devices  2.45 us (5%)
    pallas_call x3, Pallas kernels, local_level(): pl.pallas_call(local_kernel, grid=(count,), in_specs=in_specs, out_specs=...  29.9 us
    ppermute x9, starting transfers between devices, exchange(): lax.ppermute(array, 'seq', [(i, i ^ distance) for i in range(devices)])  17.5 us
    ppermute x9, waiting for transfers between devices, exchange(): lax.ppermute(array, 'seq', [(i, i ^ distance) for i in range(devices)])  2.45 us
    pallas_call x1, Pallas kernels, merge(): pl.pallas_call(merge_kernel, in_specs=[pl.BlockSpec(memory_space=pltpu.SM...  2.28 us
    pallas_call x1, Pallas kernels, pick(): pl.pallas_call(pick_kernel, grid=(1,), in_specs=[spec] * 3, out_specs=[pl...  1.63 us
  transfers between devices with their start and end apart: 9, of which 2 were waited for; matrix products, arithmetic and copies ran while one was open for 0% of the time, Pallas kernels for 55%

commit v1 on v0

--- a/solution.py
+++ b/solution.py
@@ -25,7 +25,7 @@
 F32 = jnp.float32
 TRANSPOSED = (((1,), (1,)), ((), ()))
 
-CHUNKS = (2, 5, 1)
+CHUNKS = (1, 1, 5, 1)
 
 
 def owner_mask(rows, row_size, columns):
@@ -34,7 +34,7 @@
     return row == head
 
 
-def pick_kernel(q_ref, k_ref, v_ref, q_out, own_out, second_out, fourth_out):
+def pick_kernel(q_ref, k_ref, v_ref, q_out, own_out, second_out, low_out, high_out):
     owned = owner_mask(ROWS, 1, WIDTH)
 
     def diagonal(ref):
@@ -51,8 +51,9 @@
         rows = diagonal(ref)
         none = [jnp.zeros_like(rows[0])] * (ROWS // 4)
         own_out[:, columns] = pack(rows)
-        second_out[:, columns] = pack(rows[2::4] + rows[::4])
-        fourth_out[:, columns] = pack(rows[::4] + none)
+        second_out[:, columns] = pack(rows[::2])
+        low_out[:, columns] = pack(rows[::4] + none)
+        high_out[:, columns] = pack(none + rows[::4])
 
 
 def pick(queries, key_rows, value_rows):
@@ -60,7 +61,7 @@
     shape = (ROWS, STRIDE, WIDTH)
     outs = [
         jax.ShapeDtypeStruct(size, BF16)
-        for size in ((ROWS, WIDTH), (ROWS, 2 * WIDTH)) + ((ROWS // 2, 2 * WIDTH),) * 2
+        for size in ((ROWS, WIDTH), (ROWS, 2 * WIDTH)) + ((ROWS // 2, 2 * WIDTH),) * 3
     ]
     return pl.pallas_call(
         pick_kernel,
@@ -187,9 +188,9 @@
     column = lax.broadcasted_iota(jnp.int32, (1, keys), 1)
     core, x, z = column // (keys // 2), column // (4 * UNIT) % 4, column // UNIT % 4
     inner = column % UNIT
-    quarter = jnp.where(inner < 16, 0, jnp.where(inner < 24, 1, jnp.where(inner < 28, 3, 2)))
+    quarter = jnp.where(inner < 16, 0, jnp.where(inner < 24, 1, jnp.where(inner < 28, 2, 3)))
     index = jnp.where(
-        inner < 16, inner, 4 * (inner % 4) + jnp.where((inner >= 16) & (inner < 20), 2, 0)
+        inner < 16, inner, jnp.where(inner < 24, 2 * (inner - 16), 4 * (inner % 4))
     )
     source = jnp.bitwise_xor(device, quarter * 32 + x * 8 + z * 2 + core)
     key_place = source * ROWS + index
@@ -263,21 +264,23 @@
     def exchange(array, distance):
         return lax.ppermute(array, "seq", [(i, i ^ distance) for i in range(devices)])
 
-    query, rows, second, fourth = pick(*arrays)
-    near = exchange(second, 32)
-    own = lax.broadcasted_iota(jnp.int32, second.shape, 0) < ROWS // 4
-    far = exchange(jnp.where(own, fourth, near), 96)
-    rows = jnp.concatenate([rows, near, far], 0)
+    query, rows, *sent = pick(*arrays)
     complete, kept, first = None, [], 0
-    for stage, (distances, count) in enumerate(zip(((2, 4, 6), (8, 16, 24), (1,)), CHUNKS)):
-        rows, complete, arrays = lax.optimization_barrier((rows, complete, arrays))
-        received = [exchange(rows, distance) for distance in distances]
+    stages = ((32, 64, 96), (2, 4, 6), (8, 16, 24), (1,))
+    for stage, (distances, count) in enumerate(zip(stages, CHUNKS)):
+        if stage > 0:
+            sent = [rows] * len(distances)
+        received = [exchange(part, distance) for part, distance in zip(sent, distances)]
         complete, some = local_level(first, count, arrays, complete)
         first += count
         kept.append(some)
         received, rows, complete = lax.optimization_barrier((received, rows, complete))
-        if stage < 2:
+        if stage == 0:
+            rows = jnp.concatenate([rows, received[0], received[1] + received[2]], 0)
+        elif stage < 3:
             rows = jnp.concatenate([rows, *received], 0)
+        if stage < 3:
+            rows, complete, arrays = lax.optimization_barrier((rows, complete, arrays))
     spot = lax.axis_index("seq").astype(jnp.int32).reshape(1)
     return merge(spot, query, rows, received[0], kept, complete)
 

time: 54.4 us -> 52.5 us (0.965)
  waiting for transfers between devices: 2.45 us -> 0.03 us
  Pallas kernels: 33.8 us -> 36.1 us
  starting transfers between devices: 17.5 us -> 15.8 us
    pallas_call x3 -> x4, Pallas kernels: 29.9 us -> 32.3 us  [local_level(): pl.pallas_call(local_kernel, grid=(count,), in_specs=in_specs, out_specs=...]
    ppermute x9 -> x10, waiting for transfers between devices: 2.45 us -> 0.03 us  [exchange(): lax.ppermute(array, 'seq', [(i, i ^ distance) for i in range(devices)])]
    ppermute x9 -> x10, starting transfers between devices: 17.5 us -> 15.8 us  [exchange(): lax.ppermute(array, 'seq', [(i, i ^ distance) for i in range(devices)])]
  transfers between devices with their start and end apart: 9 -> 10, of which waited for: 2 -> 0; matrix products, arithmetic and copies ran while one was open for 0% -> 0% of each run, Pallas kernels for 55% -> 62%
where the time goes in v1:
time: 52.5 us; the launch traced here: 52.3 us
  Pallas kernels  36.1 us (69%)
  starting transfers between devices  15.8 us (30%)
    pallas_call x4, Pallas kernels, local_level(): pl.pallas_call(local_kernel, grid=(count,), in_specs=in_specs, out_specs=...  32.3 us
    ppermute x10, starting transfers between devices, exchange(): lax.ppermute(array, 'seq', [(i, i ^ distance) for i in range(devices)])  15.8 us
    pallas_call x1, Pallas kernels, merge(): pl.pallas_call(merge_kernel, in_specs=[pl.BlockSpec(memory_space=pltpu.SM...  2.2 us
    pallas_call x1, Pallas kernels, pick(): pl.pallas_call(pick_kernel, grid=(1,), in_specs=[spec] * 3, out_specs=[pl...  1.63 us
  transfers between devices with their start and end apart: 10, of which 0 were waited for; matrix products, arithmetic and copies ran while one was open for 0% of the time, Pallas kernels for 62%

profile of v1, /device:TPU:1, one launch (start us, length us, event | category | flops | bytes accessed | tf_op | source)
XLA Modules:
  0.0 52.3 jit_solution(15592677953452001979)
XLA Ops:
  0.0 1.6 %pick.1 = (bf16[16,768]{1,0:T(8,128)(2,1)S(1)}, bf16[16,1536]{1,0:T(8,128)(2,1)S(1)}, bf16[8,1536]{1,0:T(8,128)(2,1)S(1)}, bf16[8,1536]{1,0:T(8,128)(2,1)S(1)}, bf16[8,1536]{1,0:T(8,128)(2,1)S(1)}) custom-call(bf16[16,256,768]{2,1,0:T(8,128)(2,1)} %bitcast.6, bf16[16,256,768]{2,1,0:T(8,128)(2,1)} %bitcast.7, bf16[16,256,768]{2,1,0:T(8,128)(2,1)} %bitcast.8), custom_call_target="tpu_custom_call" | custom-call | tf_op jit(solution)/shard_map/pick/pallas_call | solution.py:66
  1.6 2.2 %collective-permute-start = (bf16[8,1536]{1,0:T(8,128)(2,1)S(1)}, bf16[8,1536]{1,0:T(8,128)(2,1)S(1)}, u32[]{:S(2)}, u32[]{:S(2)}) collective-permute-start(bf16[8,1536]{1,0:T(8,128)(2,1)S(1)} %get-tuple-element.52), channel_id=1, source_target_pairs={{0,32},{1,33},{2,34},{3,35},{4,36},{5,37},{6,38},{7,39},{8,40},{9,... | collective-permute-start | bytes 73736 | tf_op jit(solution)/shard_map/ppermute | solution.py:265
  3.8 2.6 %collective-permute-start.1 = (bf16[8,1536]{1,0:T(8,128)(2,1)S(1)}, bf16[8,1536]{1,0:T(8,128)(2,1)S(1)}, u32[]{:S(2)}, u32[]{:S(2)}) collective-permute-start(bf16[8,1536]{1,0:T(8,128)(2,1)S(1)} %get-tuple-element.53), channel_id=1, source_target_pairs={{0,64},{1,65},{2,66},{3,67},{4,68},{5,69},{6,70},{7,71},{8,72},{9,... | collective-permute-start | bytes 73736 | tf_op jit(solution)/shard_map/ppermute | solution.py:265
  6.5 0.0 collective-permute-start.2
  6.5 5.3 %local.4 = (bf16[4096,768]{1,0:T(8,128)(2,1)}, f32[8,768]{1,0:T(8,128)S(1)}) custom-call(bf16[4096,768]{1,0:T(8,128)(2,1)} %q_ref.4, bf16[4096,768]{1,0:T(8,128)(2,1)} %k_ref.4, bf16[4096,768]{1,0:T(8,128)(2,1)} %v_ref.4), custom_call_target="tpu_custom_call" | custom-call | flops 3221225472 | bytes 3145728 | tf_op jit(solution)/shard_map/local/pallas_call | solution.py:151
  11.7 0.0 collective-permute-done
  11.7 0.0 collective-permute-done.1
  11.7 0.0 collective-permute-done.2
  11.8 3.8 %collective-permute-start.5 = (bf16[32,1536]{1,0:T(8,128)(2,1)S(1)}, bf16[32,1536]{1,0:T(8,128)(2,1)S(1)}, u32[]{:S(2)}, u32[]{:S(2)}) collective-permute-start(bf16[32,1536]{1,0:T(8,128)(2,1)S(1)} %pad_maximum_fusion.2), channel_id=1, source_target_pairs={{0,6},{1,7},{2,4},{3,5},{4,2},{5,3},{6,0},{7,1},{8,14},{9,15},{10,... | collective-permute-start | bytes 294920 | tf_op jit(solution)/shard_map/ppermute | solution.py:265
  15.6 0.0 collective-permute-start.4
  15.6 0.7 %collective-permute-start.3 = (bf16[32,1536]{1,0:T(8,128)(2,1)S(1)}, bf16[32,1536]{1,0:T(8,128)(2,1)S(1)}, u32[]{:S(2)}, u32[]{:S(2)}) collective-permute-start(bf16[32,1536]{1,0:T(8,128)(2,1)S(1)} %pad_maximum_fusion.2), channel_id=1, source_target_pairs={{0,2},{1,3},{2,0},{3,1},{4,6},{5,7},{6,4},{7,5},{8,10},{9,11},{10,... | collective-permute-start | bytes 294920 | tf_op jit(solution)/shard_map/ppermute | solution.py:265
  16.3 5.3 %local.5 = (bf16[4096,768]{1,0:T(8,128)(2,1)}, f32[8,768]{1,0:T(8,128)S(1)}) custom-call(bf16[4096,768]{1,0:T(8,128)(2,1)} %q_ref.4, bf16[4096,768]{1,0:T(8,128)(2,1)} %k_ref.4, bf16[4096,768]{1,0:T(8,128)(2,1)} %v_ref.4, bf16[4096,768]{1,0:T(8,128)(2,1)} %get-tuple-element.66.refs_0_), custom_call_target="tpu_custom_call", output_to_operand_aliasing={{0}: (3, {})} | custom-call | flops 3221225472 | bytes 3145728 | tf_op jit(solution)/shard_map/local/pallas_call | solution.py:151
  21.5 0.0 collective-permute-done.5
  21.6 0.0 collective-permute-done.4
  21.6 2.6 %collective-permute-start.8 = (bf16[128,1536]{1,0:T(8,128)(2,1)S(1)}, bf16[128,1536]{1,0:T(8,128)(2,1)S(1)}, u32[]{:S(2)}, u32[]{:S(2)}) collective-permute-start(bf16[128,1536]{1,0:T(8,128)(2,1)S(1)} %pad_maximum_fusion.1), channel_id=1, source_target_pairs={{0,24},{1,25},{2,26},{3,27},{4,28},{5,29},{6,30},{7,31},{8,16},{9,... | collective-permute-start | bytes 1179656 | tf_op jit(solution)/shard_map/ppermute | solution.py:265
  24.2 0.5 collective-permute-start.7
  24.7 0.3 collective-permute-start.6
  24.9 16.5 %local.6 = (bf16[4096,768]{1,0:T(8,128)(2,1)}, f32[40,768]{1,0:T(8,128)S(1)}) custom-call(bf16[4096,768]{1,0:T(8,128)(2,1)} %q_ref.4, bf16[4096,768]{1,0:T(8,128)(2,1)} %k_ref.4, bf16[4096,768]{1,0:T(8,128)(2,1)} %v_ref.4, bf16[4096,768]{1,0:T(8,128)(2,1)} %get-tuple-element.77.refs_0_), custom_call_target="tpu_custom_call", output_to_operand_aliasing={{0}: (3, {})} | custom-call | flops 16106127360 | bytes 15728640 | tf_op jit(solution)/shard_map/local/pallas_call | solution.py:151
  41.5 0.0 collective-permute-done.8
  41.5 0.0 collective-permute-done.7
  41.5 0.1 pad_maximum_fusion.own_ref
  41.6 3.1 %collective-permute-start.9 = (bf16[512,1536]{1,0:T(8,128)(2,1)S(1)}, bf16[512,1536]{1,0:T(8,128)(2,1)S(1)}, u32[]{:S(2)}, u32[]{:S(2)}) collective-permute-start(bf16[512,1536]{1,0:T(8,128)(2,1)S(1)} %pad_maximum_fusion.own_ref), channel_id=1, source_target_pairs={{0,1},{1,0},{2,3},{3,2},{4,5},{5,4},{6,7},{7,6},{8,9},{9,8},{10,11... | collective-permute-start | bytes 4718600 | tf_op jit(solution)/shard_map/ppermute | solution.py:265
  44.7 5.3 %local.7 = (bf16[4096,768]{1,0:T(8,128)(2,1)}, f32[8,768]{1,0:T(8,128)S(1)}) custom-call(bf16[4096,768]{1,0:T(8,128)(2,1)} %q_ref.4, bf16[4096,768]{1,0:T(8,128)(2,1)} %k_ref.4, bf16[4096,768]{1,0:T(8,128)(2,1)} %v_ref.4, bf16[4096,768]{1,0:T(8,128)(2,1)} %get-tuple-element.88.refs_0_), custom_call_target="tpu_custom_call", output_to_operand_aliasing={{0}: (3, {})} | custom-call | flops 3221225472 | bytes 3145728 | tf_op jit(solution)/shard_map/local/pallas_call | solution.py:151
  50.0 2.2 %merge.1 = bf16[16,256,768]{2,1,0:T(8,128)(2,1)} custom-call(s32[1]{0:T(128)} %bitcast.spot_ref, bf16[16,768]{1,0:T(8,128)(2,1)S(1)} %get-tuple-element.51.q_ref, bf16[512,1536]{1,0:T(8,128)(2,1)S(1)} %pad_maximum_fusion.own_ref, bf16[512,1536]{1,0:T(8,128)(2,1)S(1)} %collective-permute-done.9.other_ref, ...), custom_call_target="tpu_custom_call", output_to_operand_aliasing={{}: (8, {})} | custom-call | tf_op jit(solution)/shard_map/merge/pallas_call | solution.py:243
  (6 shorter events, 0.1 us)
Async XLA Ops:
  1.6 10.1 %collective-permute-start = (bf16[8,1536]{1,0:T(8,128)(2,1)S(1)}, bf16[8,1536]{1,0:T(8,128)(2,1)S(1)}, u32[]{:S(2)}, u32[]{:S(2)}) collective-permute-start(bf16[8,1536]{1,0:T(8,128)(2,1)S(1)} %get-tuple-element.52), channel_id=1, source_target_pairs={{0,32},{1,33},{2,34},{3,35},{4,36},{5,37},{6,38},{7,39},{8,40},{9,... | collective-permute-start | bytes 73736 | tf_op jit(solution)/shard_map/ppermute | solution.py:265
  3.8 7.9 %collective-permute-start.1 = (bf16[8,1536]{1,0:T(8,128)(2,1)S(1)}, bf16[8,1536]{1,0:T(8,128)(2,1)S(1)}, u32[]{:S(2)}, u32[]{:S(2)}) collective-permute-start(bf16[8,1536]{1,0:T(8,128)(2,1)S(1)} %get-tuple-element.53), channel_id=1, source_target_pairs={{0,64},{1,65},{2,66},{3,67},{4,68},{5,69},{6,70},{7,71},{8,72},{9,... | collective-permute-start | bytes 73736 | tf_op jit(solution)/shard_map/ppermute | solution.py:265
  6.5 5.3 %collective-permute-start.2 = (bf16[8,1536]{1,0:T(8,128)(2,1)S(1)}, bf16[8,1536]{1,0:T(8,128)(2,1)S(1)}, u32[]{:S(2)}, u32[]{:S(2)}) collective-permute-start(bf16[8,1536]{1,0:T(8,128)(2,1)S(1)} %get-tuple-element.54), channel_id=1, source_target_pairs={{0,96},{1,97},{2,98},{3,99},{4,100},{5,101},{6,102},{7,103},{8,104... | collective-permute-start | bytes 73736 | tf_op jit(solution)/shard_map/ppermute | solution.py:265
  11.8 9.8 %collective-permute-start.5 = (bf16[32,1536]{1,0:T(8,128)(2,1)S(1)}, bf16[32,1536]{1,0:T(8,128)(2,1)S(1)}, u32[]{:S(2)}, u32[]{:S(2)}) collective-permute-start(bf16[32,1536]{1,0:T(8,128)(2,1)S(1)} %pad_maximum_fusion.2), channel_id=1, source_target_pairs={{0,6},{1,7},{2,4},{3,5},{4,2},{5,3},{6,0},{7,1},{8,14},{9,15},{10,... | collective-permute-start | bytes 294920 | tf_op jit(solution)/shard_map/ppermute | solution.py:265
  15.6 5.9 %collective-permute-start.4 = (bf16[32,1536]{1,0:T(8,128)(2,1)S(1)}, bf16[32,1536]{1,0:T(8,128)(2,1)S(1)}, u32[]{:S(2)}, u32[]{:S(2)}) collective-permute-start(bf16[32,1536]{1,0:T(8,128)(2,1)S(1)} %pad_maximum_fusion.2), channel_id=1, source_target_pairs={{0,4},{1,5},{2,6},{3,7},{4,0},{5,1},{6,2},{7,3},{8,12},{9,13},{10,... | collective-permute-start | bytes 294920 | tf_op jit(solution)/shard_map/ppermute | solution.py:265
  15.6 5.9 %collective-permute-start.3 = (bf16[32,1536]{1,0:T(8,128)(2,1)S(1)}, bf16[32,1536]{1,0:T(8,128)(2,1)S(1)}, u32[]{:S(2)}, u32[]{:S(2)}) collective-permute-start(bf16[32,1536]{1,0:T(8,128)(2,1)S(1)} %pad_maximum_fusion.2), channel_id=1, source_target_pairs={{0,2},{1,3},{2,0},{3,1},{4,6},{5,7},{6,4},{7,5},{8,10},{9,11},{10,... | collective-permute-start | bytes 294920 | tf_op jit(solution)/shard_map/ppermute | solution.py:265
  21.6 19.9 %collective-permute-start.8 = (bf16[128,1536]{1,0:T(8,128)(2,1)S(1)}, bf16[128,1536]{1,0:T(8,128)(2,1)S(1)}, u32[]{:S(2)}, u32[]{:S(2)}) collective-permute-start(bf16[128,1536]{1,0:T(8,128)(2,1)S(1)} %pad_maximum_fusion.1), channel_id=1, source_target_pairs={{0,24},{1,25},{2,26},{3,27},{4,28},{5,29},{6,30},{7,31},{8,16},{9,... | collective-permute-start | bytes 1179656 | tf_op jit(solution)/shard_map/ppermute | solution.py:265
  24.2 17.3 %collective-permute-start.7 = (bf16[128,1536]{1,0:T(8,128)(2,1)S(1)}, bf16[128,1536]{1,0:T(8,128)(2,1)S(1)}, u32[]{:S(2)}, u32[]{:S(2)}) collective-permute-start(bf16[128,1536]{1,0:T(8,128)(2,1)S(1)} %pad_maximum_fusion.1), channel_id=1, source_target_pairs={{0,16},{1,17},{2,18},{3,19},{4,20},{5,21},{6,22},{7,23},{8,24},{9,... | collective-permute-start | bytes 1179656 | tf_op jit(solution)/shard_map/ppermute | solution.py:265
  24.7 16.8 %collective-permute-start.6 = (bf16[128,1536]{1,0:T(8,128)(2,1)S(1)}, bf16[128,1536]{1,0:T(8,128)(2,1)S(1)}, u32[]{:S(2)}, u32[]{:S(2)}) collective-permute-start(bf16[128,1536]{1,0:T(8,128)(2,1)S(1)} %pad_maximum_fusion.1), channel_id=1, source_target_pairs={{0,8},{1,9},{2,10},{3,11},{4,12},{5,13},{6,14},{7,15},{8,0},{9,1},... | collective-permute-start | bytes 1179656 | tf_op jit(solution)/shard_map/ppermute | solution.py:265
  41.6 8.4 %collective-permute-start.9 = (bf16[512,1536]{1,0:T(8,128)(2,1)S(1)}, bf16[512,1536]{1,0:T(8,128)(2,1)S(1)}, u32[]{:S(2)}, u32[]{:S(2)}) collective-permute-start(bf16[512,1536]{1,0:T(8,128)(2,1)S(1)} %pad_maximum_fusion.own_ref), channel_id=1, source_target_pairs={{0,1},{1,0},{2,3},{3,2},{4,5},{5,4},{6,7},{7,6},{8,9},{9,8},{10,11... | collective-permute-start | bytes 4718600 | tf_op jit(solution)/shard_map/ppermute | solution.py:265
